TPU v7x, 256 devices: a whole 4x4x8 slice. The times are simulated.
256 devices in a mesh: dp: 32 (over z, x), grp: 8 (over y, core).
Axes of the slice: x: 4, y: 4, z: 8, core: 2. Of those that a mesh axis runs over, the one named last changes fastest.
Arguments:
- byte_states: bfloat16 [32768, 1280], P('dp'), may hold values from -36 to 36
- norm_gain: float32 [1280], replicated, may hold values from 0.1 to 1.9
- patch_window: int32 [32, 1041], P('dp'), may hold values from -1 to 8192, as said below
- w_query: bfloat16 [1280, 4096], P('dp', 'grp'), may hold values from -0.11320094 to 0.11320094
- w_key: bfloat16 [1280, 4096], P('dp', 'grp'), may hold values from -9.056075 to 9.056075
- w_value: bfloat16 [1280, 4096], P('dp', 'grp'), may hold values from -0.15625 to 0.15625
- w_out: bfloat16 [4096, 4096], P('grp', 'dp'), may hold values from -0.09375 to 0.09375
- cotangent: bfloat16 [8192, 4096], P('dp', 'grp'), may hold values from -6 to 6
Outputs:
- patch_rows: bfloat16 [8192, 4096], P('dp', 'grp')
- grad_attended: float32 [8192, 4096], P('dp', 'grp')
Inputs may be any that keep to these rules, and one draw needn't show every extreme that they name: `patch_window`: row d holds the patch numbers of the 1024 bytes of dp index d, preceded by those of the 16 bytes before them (-1 before the stream) and followed by that of the next byte (8192 after the stream). Patch numbers never fall and take every value from 0 to 8191. Between 128 and 640 patches end on the bytes of one dp index, 640 on some index in every draw; those ending on the bytes of dp index d are numbered from (d - 2) * 256 to (d + 3) * 256 - 1. The first patch ending on a device's bytes begins at most 15 bytes before them, exactly so on some device in every draw.
All inputs are finite; a program needn't handle non-finite values.
Results may differ from a plain program's by a relative error of at most 0.025.
Values may be sent and summed in bfloat16 or wider, within the bound.
No kernel may reach another device: no remote copies, remote signals or barrier semaphores. Data moves between devices by JAX's collectives and lax.ppermute only.
A program may use at most 64 MiB of HBM per device.

v0:
```python
import jax
import jax.numpy as jnp
from jax import lax
from jax.sharding import PartitionSpec as P

HDIM = 128
MOST = 16
PAT_DEV = 256
PCAP = 640


EPSILON = 1e-05


def from_behind(value, axis, steps):
    count = lax.axis_size(axis)
    leading, last = (max(0, -steps), min(count, count - steps))
    return lax.ppermute(value, axis, [(source, source + steps) for source in range(leading, last)])


def normalize(states, gain):
    as_float = states.astype(jnp.float32)
    mean_square = jnp.mean(as_float * as_float, axis=1, keepdims=True)
    return (as_float * lax.rsqrt(mean_square + EPSILON) * gain).astype(jnp.bfloat16)


def arrange(source, device_index, offset, first_patch, patch_total):
    slot_index = (
        (device_index + offset) * PAT_DEV - first_patch + jnp.arange(PAT_DEV, dtype=jnp.int32)
    )
    keep_rows = (slot_index >= 0) & (slot_index < patch_total)
    picked = jnp.take(source, jnp.clip(slot_index, 0, PCAP - 1), axis=0)
    return jnp.where(keep_rows[:, None], picked, jnp.zeros_like(picked))


def per_device(byte_states, norm_gain, patch_window, w_query, w_key, w_value, w_out, cotangent):
    byte_count = byte_states.shape[0]
    columns = w_query.shape[1]
    head_count = columns // HDIM
    highest_precision = lax.Precision.HIGHEST
    normed = normalize(byte_states, norm_gain)
    before = from_behind(normed[byte_count - MOST :], "dp", 1)
    window = jnp.concatenate([before, normed], axis=0)
    span_rows = window.shape[0]
    patch_ids = patch_window[0, :span_rows]
    first_patch = patch_window[0, MOST]
    patch_total = patch_window[0, span_rows] - first_patch
    relative = patch_ids - first_patch
    owned = (relative >= 0) & (relative < patch_total)
    segment = jnp.where(owned, relative, PCAP)
    slot_numbers = jnp.arange(PCAP, dtype=jnp.int32)
    member = segment[None, :] == slot_numbers[:, None]
    member_half = member.astype(jnp.bfloat16)
    member_full = member.astype(jnp.float32)
    patch_sizes = jnp.sum(member_full, axis=1)
    byte_sums = jnp.dot(member_half, window, preferred_element_type=jnp.float32)
    pooled = (byte_sums / jnp.where(patch_sizes > 0, patch_sizes, 1.0)[:, None]).astype(
        jnp.bfloat16
    )
    query_sum = jnp.dot(
        pooled,
        lax.all_gather(w_query, "dp", axis=0, tiled=True),
        preferred_element_type=jnp.float32,
    )
    key_sum = jnp.dot(
        window, lax.all_gather(w_key, "dp", axis=0, tiled=True), preferred_element_type=jnp.float32
    )
    value_sum = jnp.dot(
        window,
        lax.all_gather(w_value, "dp", axis=0, tiled=True),
        preferred_element_type=jnp.float32,
    )
    queries = query_sum.astype(jnp.bfloat16)
    key_rows = key_sum.astype(jnp.bfloat16)
    value_rows = value_sum.astype(jnp.bfloat16)
    query_rows = lax.dot_general(
        member_half, queries, (((0,), (0,)), ((), ())), preferred_element_type=jnp.float32
    )
    product = query_rows * key_rows.astype(jnp.float32)
    scores = product.reshape(span_rows, head_count, HDIM).sum(axis=2) * HDIM ** (-0.5)
    highest = jnp.max(jnp.where(member[:, :, None], scores[None, :, :], -1e30), axis=1)
    highest_rows = lax.dot_general(
        member_full,
        highest,
        (((0,), (0,)), ((), ())),
        precision=highest_precision,
        preferred_element_type=jnp.float32,
    )
    weights = jnp.exp(jnp.where(owned[:, None], scores - highest_rows, -1e30))
    totals = jnp.dot(
        member_full, weights, precision=highest_precision, preferred_element_type=jnp.float32
    )
    weighted = weights[:, :, None] * value_rows.astype(jnp.float32).reshape(
        span_rows, head_count, HDIM
    )
    sums = jnp.dot(
        member_full,
        weighted.reshape(span_rows, columns),
        precision=highest_precision,
        preferred_element_type=jnp.float32,
    )
    result = sums.reshape(PCAP, head_count, HDIM) / jnp.where(totals > 0, totals, 1.0)[:, :, None]
    attended = result.reshape(PCAP, columns).astype(jnp.bfloat16)
    weight_full = lax.all_gather(w_out, "dp", axis=1, tiled=True)
    device_index = lax.axis_index("dp")
    terms = jnp.dot(attended, weight_full, preferred_element_type=jnp.float32)
    mixed_rows = lax.psum_scatter(
        terms.astype(jnp.bfloat16), "grp", scatter_dimension=1, tiled=True
    ).astype(jnp.float32)
    patch_local = (queries.astype(jnp.float32) + mixed_rows).astype(jnp.bfloat16)
    landed = arrange(patch_local, device_index, 0, first_patch, patch_total).astype(jnp.float32)
    for offset in (-2, -1, 1, 2):
        arrived = from_behind(
            arrange(patch_local, device_index, offset, first_patch, patch_total), "dp", offset
        )
        landed = landed + arrived.astype(jnp.float32)
    patch_rows = landed.astype(jnp.bfloat16)
    gradient = lax.dot_general(
        lax.all_gather(cotangent, "grp", axis=1, tiled=True),
        weight_full,
        (((1,), (1,)), ((), ())),
        preferred_element_type=jnp.float32,
    )
    return (patch_rows, gradient)


def solution(mesh):
    return jax.shard_map(
        per_device,
        mesh=mesh,
        in_specs=(
            P("dp", None),
            P(),
            P("dp", None),
            P("dp", "grp"),
            P("dp", "grp"),
            P("dp", "grp"),
            P("grp", "dp"),
            P("dp", "grp"),
        ),
        out_specs=(P("dp", "grp"), P("dp", "grp")),
        check_vma=False,
    )
```

profile of v0, /device:TPU:6, one launch (start us, length us, event | category | flops | bytes accessed | tf_op | source)
XLA Modules:
  0.0 420.4 jit_solution(66476593252226897)
XLA Ops:
  7.2 0.7 all-gather.6.cloned.1.call-update
  8.0 0.7 all-gather.8.cloned.1.call-update
  8.7 0.7 all-gather.10.cloned.1.call-update
  9.4 0.5 all-gather.12.cloned.1.call-update
  10.0 2.3 fusion
  12.4 0.7 fusion.2
  13.1 1.5 copy-done.1
  14.6 3.7 collective-permute-start
  18.4 0.6 fusion.34
  20.2 0.7 select_reduce_fusion.1
  20.9 0.3 convert_reduce_fusion
  21.3 0.4 iota_compare_fusion
  21.7 0.7 fusion.29
  22.4 66.7 %all-gather.6.cloned.1.call-done = bf16[1280,512]{1,0:T(8,128)(2,1)} async-done(((bf16[40,512]{1,0:T(8,128)(2,1)}), bf16[1280,512]{1,0:T(8,128)(2,1)}) %all-gather.6.cloned.1.call-update) | async-done | bytes 1310736 | tf_op jit(solution)/shard_map/all_gather | solution.py:62
  89.2 6.3 %convolution_convert_fusion.3 = bf16[640,512]{1,0:T(8,128)(2,1)} fusion(bf16[1280,512]{1,0:T(8,128)(2,1)} %all-gather.6.cloned.1.call-done, f32[640]{0:T(1024)S(1)} %compare_select_fusion.1, s32[1040]{0:T(1024)S(1)} %select_reduce_fusion.1, bf16[1024,1280]{1,0:T(8,128)(2,1)} %copy-done.1, bf16[16,1280]{1,0:T(8,128)(2,1)S(1)} %collective-permute-done), kind=kOutput, calls=%fused_computation.34 | convolution fusion | flops 2550753280 | bytes 4635200 | tf_op jit(solution)/shard_map/dot_general | solution.py:60
  95.5 3.6 fusion.11
  99.0 67.0 %all-gather.8.cloned.1.call-done = bf16[1280,512]{1,0:T(8,128)(2,1)} async-done(((bf16[40,512]{1,0:T(8,128)(2,1)}), bf16[1280,512]{1,0:T(8,128)(2,1)}) %all-gather.8.cloned.1.call-update) | async-done | bytes 1310736 | tf_op jit(solution)/shard_map/all_gather | solution.py:66
  166.1 4.8 %fusion.7 = f32[1040,512]{1,0:T(8,128)} fusion(f32[1040,512]{1,0:T(8,128)} %fusion.11, bf16[1280,512]{1,0:T(8,128)(2,1)} %all-gather.8.cloned.1.call-done, bf16[1024,1280]{1,0:T(8,128)(2,1)S(1)} %copy-done.2, bf16[16,1280]{1,0:T(8,128)(2,1)S(1)} %collective-permute-done), kind=kOutput, calls=%fused_computation.19 | convolution fusion | flops 1370071040 | bytes 8232960 | tf_op jit(solution)/shard_map/dot_general | solution.py:65
  170.9 2.4 reshape.107
  173.3 1.8 reduce_sum.29
  175.1 0.2 copy.19
  175.4 1.0 select_reduce_fusion
  176.3 1.3 fusion.16
  177.7 0.2 copy.20
  177.9 1.0 compare_select_fusion
  178.9 64.1 %all-gather.10.cloned.1.call-done = bf16[1280,512]{1,0:T(8,128)(2,1)} async-done(((bf16[40,512]{1,0:T(8,128)(2,1)}), bf16[1280,512]{1,0:T(8,128)(2,1)}) %all-gather.10.cloned.1.call-update) | async-done | bytes 1310736 | tf_op jit(solution)/shard_map/all_gather | solution.py:70
  243.0 2.4 mul.67
  245.4 1.5 fusion.19
  247.0 3.6 divide_convert_fusion
  250.5 77.3 %all-gather.12.cloned.1.call-done = bf16[512,4096]{1,0:T(8,128)(2,1)} async-done(((bf16[512,128]{1,0:T(8,128)(2,1)}), bf16[512,4096]{1,0:T(8,128)(2,1)}) %all-gather.12.cloned.1.call-update) | async-done | bytes 4194320 | tf_op jit(solution)/shard_map/all_gather | solution.py:104
  327.9 7.4 %convolution_convert_fusion = bf16[640,4096]{1,0:T(8,128)(2,1)} fusion(bf16[640,512]{0,1:T(8,128)(2,1)S(1)} %bitcast.32, bf16[512,4096]{1,0:T(8,128)(2,1)} %all-gather.12.cloned.1.call-done), kind=kOutput, calls=%fused_computation.8 | convolution fusion | flops 2686976000 | bytes 10092544 | tf_op jit(solution)/shard_map/dot_general | solution.py:106
  335.3 0.3 all-gather.14.cloned.1.call-start
  335.6 0.3 all-gather.14.cloned.1.call-update
  339.4 38.1 %reduce-scatter.2.cloned.1.call-done = bf16[640,512]{1,0:T(8,128)(2,1)} async-done(((bf16[640,4096]{1,0:T(8,128)(2,1)}), bf16[640,512]{1,0:T(8,128)(2,1)}) %reduce-scatter.2.cloned.1.call-update) | async-done | bytes 655376 | tf_op jit(solution)/shard_map/reduce_scatter | solution.py:107
  377.5 1.3 add_convert_fusion
  378.7 1.2 gather_fusion.1
  379.9 0.1 select_select_fusion.3
  380.0 3.4 collective-permute-start.1
  383.4 1.2 gather_fusion.2
  384.7 1.9 collective-permute-start.2
  386.6 1.2 gather_fusion.3
  387.9 6.0 %collective-permute-start.3 = (bf16[256,512]{1,0:T(8,128)(2,1)S(1)}, bf16[256,512]{1,0:T(8,128)(2,1)S(1)}, u32[]{:S(2)}, u32[]{:S(2)}) collective-permute-start(bf16[256,512]{1,0:T(8,128)(2,1)S(1)} %select_select_fusion.1), channel_id=1, source_target_pairs={{0,8},{8,16},{16,24},{24,32},{32,40},{40,48},{48,56},{56,64},{64,7... | collective-permute-start | bytes 786440 | tf_op jit(solution)/shard_map/ppermute | solution.py:18
  394.0 1.2 gather_fusion.4
  395.3 2.8 collective-permute-start.4
  398.0 8.4 %all-gather.14.cloned.1.call-done = bf16[256,4096]{1,0:T(8,128)(2,1)} async-done(((bf16[256,512]{1,0:T(8,128)(2,1)}), bf16[256,4096]{1,0:T(8,128)(2,1)}) %all-gather.14.cloned.1.call-update) | async-done | bytes 2097168 | tf_op jit(solution)/shard_map/all_gather | solution.py:119
  406.5 4.9 %fusion.35 = f32[256,512]{1,0:T(8,128)} fusion(bf16[256,4096]{1,0:T(8,128)(2,1)} %all-gather.14.cloned.1.call-done, bf16[512,4096]{1,0:T(8,128)(2,1)} %all-gather.12.cloned.1.call-done), kind=kOutput, calls=%fused_computation.85 | convolution fusion | flops 1073741824 | bytes 6815744 | tf_op jit(solution)/shard_map/dot_general | solution.py:118
  411.4 1.2 gather_fusion
  412.6 1.0 add_convert_fusion.1
  (48 shorter events, 0.8 us)
Async XLA Ops:
  7.2 5.2 %copy-start = (bf16[1024,1280]{1,0:T(8,128)(2,1)S(1)}, bf16[1024,1280]{1,0:T(8,128)(2,1)}, u32[]{:S(2)}) copy-start(bf16[1024,1280]{1,0:T(8,128)(2,1)} %param.10) | copy-start | bytes 7864324
  7.2 5.2 %copy-start.6 = (f32[1280]{0:T(1024)S(1)}, f32[1280]{0:T(1024)}, u32[]{:S(2)}) copy-start(f32[1280]{0:T(1024)} %param.11) | copy-start | bytes 15364
  7.2 82.0 %all-gather.6.cloned.1.call-start = ((), (), s32[]{:S(2)}) async-start(), calls=%async_computation.1 | async-start | bytes 1351680 | tf_op jit(solution)/shard_map/all_gather | solution.py:62
  7.9 158.2 %all-gather.8.cloned.1.call-start = ((), (), s32[]{:S(2)}) async-start(), calls=%async_computation.2 | async-start | bytes 1351680 | tf_op jit(solution)/shard_map/all_gather | solution.py:66
  8.7 234.3 %all-gather.10.cloned.1.call-start = ((), (), s32[]{:S(2)}) async-start(), calls=%async_computation.3 | async-start | bytes 1351680 | tf_op jit(solution)/shard_map/all_gather | solution.py:70
  9.4 318.5 %all-gather.12.cloned.1.call-start = ((), (), s32[]{:S(2)}) async-start(), calls=%async_computation.4 | async-start | bytes 4325376 | tf_op jit(solution)/shard_map/all_gather | solution.py:104
  10.0 367.5 %reduce-scatter.2.cloned.1.call-start = ((), (), s32[]{:S(2)}) async-start(), calls=%async_computation.5 | async-start | bytes 5898240 | tf_op jit(solution)/shard_map/reduce_scatter | solution.py:107
  12.4 6.0 %copy-start.5 = (s32[1,1041]{1,0:T(1,128)S(1)}, s32[1,1041]{1,0:T(1,128)}, u32[]{:S(2)}) copy-start(s32[1,1041]{1,0:T(1,128)} %param.12) | copy-start | bytes 12496
  13.1 1.5 copy-start.1
  14.6 7.8 %collective-permute-start = (bf16[16,1280]{1,0:T(8,128)(2,1)S(1)}, bf16[16,1280]{1,0:T(8,128)(2,1)S(1)}, u32[]{:S(2)}, u32[]{:S(2)}) collective-permute-start(bf16[16,1280]{1,0:T(8,128)(2,1)S(1)} %slice.26), channel_id=1, source_target_pairs={{0,8},{8,16},{16,24},{24,32},{32,40},{40,48},{48,56},{56,64},{64,7... | collective-permute-start | bytes 122888 | tf_op jit(solution)/shard_map/ppermute | solution.py:18
  95.5 70.6 %copy-start.2 = (bf16[1024,1280]{1,0:T(8,128)(2,1)S(1)}, bf16[1024,1280]{1,0:T(8,128)(2,1)}, u32[]{:S(2)}) copy-start(bf16[1024,1280]{1,0:T(8,128)(2,1)} %copy-done.1) | copy-start | bytes 7864324
  175.4 70.0 %copy-start.3 = (bf16[1024,1280]{1,0:T(8,128)(2,1)S(1)}, bf16[1024,1280]{1,0:T(8,128)(2,1)}, u32[]{:S(2)}) copy-start(bf16[1024,1280]{1,0:T(8,128)(2,1)} %copy-done.1) | copy-start | bytes 7864324
  243.0 2.4 copy-start.7
  335.3 42.2 %copy-start.4 = (bf16[640,512]{1,0:T(8,128)(2,1)S(1)}, bf16[640,512]{1,0:T(8,128)(2,1)}, u32[]{:S(2)}) copy-start(bf16[640,512]{1,0:T(8,128)(2,1)} %convolution_convert_fusion.3) | copy-start | bytes 1966084
  335.3 71.2 %all-gather.14.cloned.1.call-start = ((), (), s32[]{:S(2)}) async-start(), calls=%async_computation.6 | async-start | bytes 2359296 | tf_op jit(solution)/shard_map/all_gather | solution.py:119
  380.0 32.5 %collective-permute-start.1 = (bf16[256,512]{1,0:T(8,128)(2,1)S(1)}, bf16[256,512]{1,0:T(8,128)(2,1)S(1)}, u32[]{:S(2)}, u32[]{:S(2)}) collective-permute-start(bf16[256,512]{1,0:T(8,128)(2,1)S(1)} %select_select_fusion.3), channel_id=1, source_target_pairs={{16,0},{24,8},{32,16},{40,24},{48,32},{56,40},{64,48},{72,56},{80,... | collective-permute-start | bytes 786440 | tf_op jit(solution)/shard_map/ppermute | solution.py:18
  384.7 27.8 %collective-permute-start.2 = (bf16[256,512]{1,0:T(8,128)(2,1)S(1)}, bf16[256,512]{1,0:T(8,128)(2,1)S(1)}, u32[]{:S(2)}, u32[]{:S(2)}) collective-permute-start(bf16[256,512]{1,0:T(8,128)(2,1)S(1)} %select_select_fusion.2), channel_id=1, source_target_pairs={{8,0},{16,8},{24,16},{32,24},{40,32},{48,40},{56,48},{64,56},{72,6... | collective-permute-start | bytes 786440 | tf_op jit(solution)/shard_map/ppermute | solution.py:18
  387.9 24.6 %collective-permute-start.3 = (bf16[256,512]{1,0:T(8,128)(2,1)S(1)}, bf16[256,512]{1,0:T(8,128)(2,1)S(1)}, u32[]{:S(2)}, u32[]{:S(2)}) collective-permute-start(bf16[256,512]{1,0:T(8,128)(2,1)S(1)} %select_select_fusion.1), channel_id=1, source_target_pairs={{0,8},{8,16},{16,24},{24,32},{32,40},{40,48},{48,56},{56,64},{64,7... | collective-permute-start | bytes 786440 | tf_op jit(solution)/shard_map/ppermute | solution.py:18
  395.3 17.3 %collective-permute-start.4 = (bf16[256,512]{1,0:T(8,128)(2,1)S(1)}, bf16[256,512]{1,0:T(8,128)(2,1)S(1)}, u32[]{:S(2)}, u32[]{:S(2)}) collective-permute-start(bf16[256,512]{1,0:T(8,128)(2,1)S(1)} %select_select_fusion), channel_id=1, source_target_pairs={{0,16},{8,24},{16,32},{24,40},{32,48},{40,56},{48,64},{56,72},{64,... | collective-permute-start | bytes 786440 | tf_op jit(solution)/shard_map/ppermute | solution.py:18
Sparse Core Ops, SparseCore 0:
  10.6 78.5 all-gather.5
  91.7 74.2 all-gather.7
  168.7 74.2 all-gather.9
  245.3 82.5 all-gather.11
  335.5 41.9 reduce-scatter.1
  379.2 27.2 all-gather.13
where the time goes:
time: 422 us; the launch traced here: 420 us
  waiting for transfers between devices  325 us (77%)
  matrix products  34.5 us (8%)
  between operations  19.1 us (5%)
  starting transfers between devices  18.3 us (4%)
  local copies, waits for them, and re-layouts  13.1 us (3%)
  other arithmetic  10.8 us (3%)
    all_gather x1, waiting for transfers between devices, per_device(): weight_full = lax.all_gather(w_out, 'dp', axis=1, tiled=True)  77.3 us
    all_gather x1, waiting for transfers between devices, per_device(): lax.all_gather(w_key, 'dp', axis=0, tiled=True)  67 us
    all_gather x1, waiting for transfers between devices, per_device(): lax.all_gather(w_query, 'dp', axis=0, tiled=True)  66.7 us
    all_gather x1, waiting for transfers between devices, per_device(): lax.all_gather(w_value, 'dp', axis=0, tiled=True)  64.1 us
    reduce_scatter x1, waiting for transfers between devices, per_device(): lax.psum_scatter(terms.astype(jnp.bfloat16), 'grp', scatter_dimension=1,...  38.1 us
    ppermute x5, starting transfers between devices, from_behind(): lax.ppermute(value, axis, [(source, source + steps) for source in range(l...  17.8 us
    all_gather x1, waiting for transfers between devices, per_device(): lax.all_gather(cotangent, 'grp', axis=1, tiled=True)  8.45 us
  transfers between devices with their start and end apart: 11, of which 6 were waited for; matrix products, arithmetic and copies ran while one was open for 12% of the time, Pallas kernels for 0%

commit v1 on v0

v1 whole, which is shorter than its diff:
```python
import jax
import jax.numpy as jnp
from jax import lax
from jax.sharding import Mesh, PartitionSpec as P

HDIM = 128
MOST = 16
PAT_DEV = 256
PCAP = 640
EPSILON = 1e-05
DP = ("z", "x")
GRP = ("y", "c")


def ring(value, axis, steps):
    count = lax.axis_size(axis)
    return lax.ppermute(value, axis, [(i, (i + steps) % count) for i in range(count)])


def from_behind(value, steps):
    count = lax.axis_size(DP)
    leading, last = (max(0, -steps), min(count, count - steps))
    return lax.ppermute(value, DP, [(source, source + steps) for source in range(leading, last)])


def normalize(states, gain):
    as_float = states.astype(jnp.float32)
    mean_square = jnp.mean(as_float * as_float, axis=1, keepdims=True)
    return (as_float * lax.rsqrt(mean_square + EPSILON) * gain).astype(jnp.bfloat16)


def place(buffer, block, index, dim):
    return lax.dynamic_update_slice_in_dim(buffer, jnp.expand_dims(block, dim), index, dim)


def gather_x(block):
    me = lax.axis_index("x")
    count = lax.axis_size("x")
    arrived = [ring(block, "x", steps) for steps in range(1, count)]
    out = place(jnp.zeros((count,) + block.shape, block.dtype), block, me, 0)
    for steps, piece in enumerate(arrived, 1):
        out = place(out, piece, (me - steps) % count, 0)
    return out


def gather_z(block):
    me = lax.axis_index("z")
    count = lax.axis_size("z")
    out = place(jnp.zeros((count,) + block.shape, block.dtype), block, me, 0)
    up = down = block
    for steps in range(1, count // 2):
        up = ring(up, "z", 1)
        down = ring(down, "z", -1)
        out = place(out, up, (me - steps) % count, 0)
        out = place(out, down, (me + steps) % count, 0)
    half = block.shape[-1] // 2
    first = ring(up[..., :half], "z", 1)
    second = ring(down[..., half:], "z", -1)
    last = jnp.concatenate([first, second], axis=-1)
    return place(out, last, (me + count // 2) % count, 0)


def per_device(byte_states, norm_gain, patch_window, w_query, w_key, w_value, w_out, cotangent):
    byte_count = byte_states.shape[0]
    columns = w_query.shape[1]
    width = byte_states.shape[1]
    head_count = columns // HDIM
    highest_precision = lax.Precision.HIGHEST
    weight_full = lax.all_gather(w_out.T, DP, axis=0, tiled=True)
    packed = jnp.concatenate([w_query, w_key, w_value], axis=1)
    half = packed.shape[1] // 2
    rows = packed.shape[0]
    left = gather_z(gather_x(packed[:, :half]))
    right = gather_z(packed[:, half:])
    right = gather_x(right).transpose(1, 0, 2, 3)
    left = left.reshape(width, half)
    right = right.reshape(width, half)

    normed = normalize(byte_states, norm_gain)
    before = from_behind(normed[byte_count - MOST :], 1)
    window = jnp.concatenate([before, normed], axis=0)
    span_rows = window.shape[0]
    patch_ids = patch_window[0, :span_rows]
    first_patch = patch_window[0, MOST]
    patch_total = patch_window[0, span_rows] - first_patch
    relative = patch_ids - first_patch
    owned = (relative >= 0) & (relative < patch_total)
    segment = jnp.where(owned, relative, PCAP)
    slot_numbers = jnp.arange(PCAP, dtype=jnp.int32)
    member = segment[None, :] == slot_numbers[:, None]
    member_half = member.astype(jnp.bfloat16)
    member_full = member.astype(jnp.float32)
    patch_sizes = jnp.sum(member_full, axis=1)
    byte_sums = jnp.dot(member_half, window, preferred_element_type=jnp.float32)
    pooled = (byte_sums / jnp.where(patch_sizes > 0, patch_sizes, 1.0)[:, None]).astype(
        jnp.bfloat16
    )
    device_index = lax.axis_index(DP)
    landing = (
        (device_index - 2) * PAT_DEV - first_patch + jnp.arange(5 * PAT_DEV, dtype=jnp.int32)
    )
    chosen = (landing[:, None] == slot_numbers[None, :]).astype(jnp.bfloat16)

    queries = jnp.dot(pooled, left[:, :columns], preferred_element_type=jnp.float32).astype(
        jnp.bfloat16
    )
    key_part = jnp.dot(window, left[:, columns:], preferred_element_type=jnp.float32)
    rest = jnp.dot(window, right, preferred_element_type=jnp.float32)
    split = 2 * columns - half
    key_rows = jnp.concatenate([key_part, rest[:, :split]], axis=1).astype(jnp.bfloat16)
    value_rows = rest[:, split:].astype(jnp.bfloat16)
    query_rows = lax.dot_general(
        member_half, queries, (((0,), (0,)), ((), ())), preferred_element_type=jnp.float32
    )
    product = query_rows * key_rows.astype(jnp.float32)
    scores = product.reshape(span_rows, head_count, HDIM).sum(axis=2) * HDIM ** (-0.5)
    highest = jnp.max(jnp.where(member[:, :, None], scores[None, :, :], -1e30), axis=1)
    highest_rows = lax.dot_general(
        member_full,
        highest,
        (((0,), (0,)), ((), ())),
        precision=highest_precision,
        preferred_element_type=jnp.float32,
    )
    weights = jnp.exp(jnp.where(owned[:, None], scores - highest_rows, -1e30))
    totals = jnp.dot(
        member_full, weights, precision=highest_precision, preferred_element_type=jnp.float32
    )
    weighted = weights[:, :, None] * value_rows.astype(jnp.float32).reshape(
        span_rows, head_count, HDIM
    )
    weighted = weighted.reshape(span_rows, columns)
    high = weighted.astype(jnp.bfloat16)
    low = (weighted - high.astype(jnp.float32)).astype(jnp.bfloat16)
    sums = jnp.dot(member_half, high, preferred_element_type=jnp.float32) + jnp.dot(
        member_half, low, preferred_element_type=jnp.float32
    )
    result = sums.reshape(PCAP, head_count, HDIM) / jnp.where(totals > 0, totals, 1.0)[:, :, None]
    attended = result.reshape(PCAP, columns).astype(jnp.bfloat16)

    def rehome(source):
        spread = jnp.dot(chosen, source, preferred_element_type=jnp.float32).astype(jnp.bfloat16)
        spread = spread.reshape(5, PAT_DEV, columns)
        landed = spread[2].astype(jnp.float32)
        for offset in (-2, -1, 1, 2):
            landed = landed + from_behind(spread[offset + 2], offset).astype(jnp.float32)
        return landed

    attended_home = rehome(attended).astype(jnp.bfloat16)
    queries_home = rehome(queries)
    terms = lax.dot_general(
        attended_home, weight_full, (((1,), (1,)), ((), ())), preferred_element_type=jnp.float32
    )
    mixed_rows = lax.psum_scatter(
        terms.astype(jnp.bfloat16), GRP, scatter_dimension=1, tiled=True
    ).astype(jnp.float32)
    patch_rows = (queries_home + mixed_rows).astype(jnp.bfloat16)
    gradient = jnp.dot(
        lax.all_gather(cotangent, GRP, axis=1, tiled=True),
        weight_full,
        preferred_element_type=jnp.float32,
    )
    return (patch_rows, gradient)


def solution(mesh):
    fine = Mesh(mesh.devices.reshape(8, 4, 4, 2), DP + GRP)
    return jax.shard_map(
        per_device,
        mesh=fine,
        in_specs=(
            P(DP, None),
            P(),
            P(DP, None),
            P(DP, GRP),
            P(DP, GRP),
            P(DP, GRP),
            P(GRP, DP),
            P(DP, GRP),
        ),
        out_specs=(P(DP, GRP), P(DP, GRP)),
        check_vma=False,
    )
```

time: 422 us -> 234 us (0.55)
  waiting for transfers between devices: 325 us -> 44.9 us
  starting transfers between devices: 18.3 us -> 88.8 us
  local copies, waits for them, and re-layouts: 13.1 us -> 29.5 us
  other arithmetic: 10.8 us -> 16 us
    all_gather x5 -> x2, waiting for transfers between devices: 284 us -> 0.02 us  [the longest x1 0.02 us: per_device(): lax.all_gather(cotangent, GRP, axis=1, tiled=True)]
    ppermute x5 -> x31, starting transfers between devices: 17.8 us -> 88.7 us  [the longest x22 57.1 us: ring(): lax.ppermute(value, axis, [(i, (i + steps) % count) for i in range(count)])]
    ppermute x5 -> x31, waiting for transfers between devices: 0.01 us -> 25.2 us  [the longest x22 19 us: ring(): lax.ppermute(value, axis, [(i, (i + steps) % count) for i in range(count)])]
    reduce_scatter x1, waiting for transfers between devices: 38.1 us -> 19 us  [per_device(): lax.psum_scatter(terms.astype(jnp.bfloat16), GRP, scatter_dimension=1, ti...]
    dynamic_update_slice x0 -> x20, local copies, waits for them, and re-layouts: none -> 14.2 us  [place(): lax.dynamic_update_slice_in_dim(buffer, jnp.expand_dims(block, dim), inde...]
    gather x5 -> x0, local copies, waits for them, and re-layouts: 5.76 us -> none  [arrange(): picked = jnp.take(source, jnp.clip(slot_index, 0, PCAP - 1), axis=0)]
    dot_general x6 -> x8, matrix products: 28.6 us -> 29.6 us  [the longest x2 6.21 us: rehome(): jnp.dot(chosen, source, preferred_element_type=jnp.float32)]
  transfers between devices with their start and end apart: 11 -> 34, of which waited for: 6 -> 11; matrix products, arithmetic and copies ran while one was open for 12% -> 33% of each run, Pallas kernels for 0% -> 0%
where the time goes in v1:
time: 234 us; the launch traced here: 230 us
  starting transfers between devices  88.8 us (38%)
  waiting for transfers between devices  44.9 us (19%)
  matrix products  34.4 us (15%)
  local copies, waits for them, and re-layouts  29.5 us (13%)
  between operations  16.4 us (7%)
  other arithmetic  16 us (7%)
    ppermute x22, starting transfers between devices, ring(): lax.ppermute(value, axis, [(i, (i + steps) % count) for i in range(count)])  57.1 us
    ppermute x9, starting transfers between devices, from_behind(): lax.ppermute(value, DP, [(source, source + steps) for source in range(lea...  31.6 us
    ppermute x22, waiting for transfers between devices, ring(): lax.ppermute(value, axis, [(i, (i + steps) % count) for i in range(count)])  19 us
    reduce_scatter x1, waiting for transfers between devices, per_device(): lax.psum_scatter(terms.astype(jnp.bfloat16), GRP, scatter_dimension=1, ti...  19 us
    dynamic_update_slice x20, local copies, waits for them, and re-layouts, place(): lax.dynamic_update_slice_in_dim(buffer, jnp.expand_dims(block, dim), inde...  14.2 us
    dot_general x2, matrix products, rehome(): jnp.dot(chosen, source, preferred_element_type=jnp.float32)  6.21 us
    ppermute x9, waiting for transfers between devices, from_behind(): lax.ppermute(value, DP, [(source, source + steps) for source in range(lea...  6.19 us
    dot_general x1, matrix products, per_device(): jnp.dot(pooled, left[:, :columns], preferred_element_type=jnp.float32)  5.57 us
  transfers between devices with their start and end apart: 34, of which 11 were waited for; matrix products, arithmetic and copies ran while one was open for 33% of the time, Pallas kernels for 0%

profile of v1, /device:TPU:6, one launch (start us, length us, event | category | flops | bytes accessed | tf_op | source)
XLA Modules:
  0.0 230.0 jit_solution(8780175913512847691)
XLA Ops:
  8.8 1.7 bitcast_dynamic-update-slice_fusion.17
  10.5 1.9 collective-permute-start.16
  12.4 3.9 %collective-permute-start.17 = (bf16[40,768]{1,0:T(8,128)(2,1)}, bf16[40,768]{1,0:T(8,128)(2,1)}, u32[]{:S(2)}, u32[]{:S(2)}) collective-permute-start(bf16[40,768]{1,0:T(8,128)(2,1)} %get-tuple-element.3), channel_id=1, source_target_pairs={{0,224},{32,0},{64,32},{96,64},{128,96},{160,128},{192,160},{224,1... | collective-permute-start | bytes 184328 | tf_op jit(solution)/shard_map/ppermute | solution.py:17
  16.8 2.4 %collective-permute-start.2 = (bf16[40,768]{1,0:T(8,128)(2,1)}, bf16[40,768]{1,0:T(8,128)(2,1)}, u32[]{:S(2)}, u32[]{:S(2)}) collective-permute-start(bf16[40,768]{1,0:T(8,128)(2,1)} %get-tuple-element.15), channel_id=1, source_target_pairs={{0,16},{8,24},{16,0},{24,8},{1,17},{9,25},{17,1},{25,9},{2,18},{10... | collective-permute-start | bytes 184328 | tf_op jit(solution)/shard_map/ppermute | solution.py:17
  25.2 2.4 %fusion = f32[1024]{0:T(1024)S(1)} fusion(bf16[1024,1280]{1,0:T(8,128)(2,1)} %param.8), kind=kLoop, calls=%fused_computation.3 | loop fusion | flops 3931136 | bytes 2625536 | tf_op jit(solution)/shard_map/reduce_sum | solution.py:28
  29.0 1.5 copy-done.1
  32.4 2.7 %collective-permute-start = (bf16[16,1280]{1,0:T(8,128)(2,1)}, bf16[16,1280]{1,0:T(8,128)(2,1)S(1)}, u32[]{:S(2)}, u32[]{:S(2)}) collective-permute-start(bf16[16,1280]{1,0:T(8,128)(2,1)} %slice.110), channel_id=1, source_target_pairs={{0,8},{8,16},{16,24},{24,32},{32,40},{40,48},{48,56},{56,64},{64,7... | collective-permute-start | bytes 122888 | tf_op jit(solution)/shard_map/ppermute | solution.py:23
  37.6 1.9 collective-permute-start.4
  40.8 1.5 broadcast_in_dim.142
  43.0 1.7 collective-permute-start.18
  44.7 1.6 collective-permute-start.19
  46.3 1.5 bitcast_dynamic-update-slice_fusion.16
  47.7 1.5 bitcast_dynamic-update-slice_fusion.15
  49.2 1.7 collective-permute-start.20
  50.9 1.5 collective-permute-start.21
  55.4 2.8 %collective-permute-start.23 = (bf16[40,384]{1,0:T(8,128)(2,1)S(1)}, bf16[40,384]{1,0:T(8,128)(2,1)S(1)}, u32[]{:S(2)}, u32[]{:S(2)}) collective-permute-start(bf16[40,384]{1,0:T(8,128)(2,1)S(1)} %slice.121), channel_id=1, source_target_pairs={{0,224},{32,0},{64,32},{96,64},{128,96},{160,128},{192,160},{224,1... | collective-permute-start | bytes 92168 | tf_op jit(solution)/shard_map/ppermute | solution.py:17
  60.4 3.0 %collective-permute-start.24 = (bf16[8,40,768]{2,1,0:T(8,128)(2,1)}, bf16[8,40,768]{2,1,0:T(8,128)(2,1)S(1)}, u32[]{:S(2)}, u32[]{:S(2)}) collective-permute-start(bf16[8,40,768]{2,1,0:T(8,128)(2,1)} %fusion.37), channel_id=1, source_target_pairs={{0,8},{8,16},{16,24},{24,0},{1,9},{9,17},{17,25},{25,1},{2,10},{10... | collective-permute-start | bytes 1474568 | tf_op jit(solution)/shard_map/ppermute | solution.py:17
  65.8 3.5 %collective-permute-start.7 = (bf16[4,40,768]{2,1,0:T(8,128)(2,1)S(1)}, bf16[4,40,768]{2,1,0:T(8,128)(2,1)S(1)}, u32[]{:S(2)}, u32[]{:S(2)}) collective-permute-start(bf16[4,40,768]{2,1,0:T(8,128)(2,1)S(1)} %collective-permute-done.5), channel_id=1, source_target_pairs={{0,224},{32,0},{64,32},{96,64},{128,96},{160,128},{192,160},{224,1... | collective-permute-start | bytes 737288 | tf_op jit(solution)/shard_map/ppermute | solution.py:17
  70.1 2.9 %collective-permute-done.6 = bf16[4,40,768]{2,1,0:T(8,128)(2,1)S(1)} collective-permute-done((bf16[4,40,768]{2,1,0:T(8,128)(2,1)S(1)}, bf16[4,40,768]{2,1,0:T(8,128)(2,1)S(1)}, u32[]{:S(2)}, u32[]{:S(2)}) %collective-permute-start.6) | collective-permute-done | bytes 245792 | tf_op jit(solution)/shard_map/ppermute | solution.py:17
  74.0 2.6 %collective-permute-done.7 = bf16[4,40,768]{2,1,0:T(8,128)(2,1)S(1)} collective-permute-done((bf16[4,40,768]{2,1,0:T(8,128)(2,1)S(1)}, bf16[4,40,768]{2,1,0:T(8,128)(2,1)S(1)}, u32[]{:S(2)}, u32[]{:S(2)}) %collective-permute-start.7) | collective-permute-done | bytes 245792 | tf_op jit(solution)/shard_map/ppermute | solution.py:17
  76.7 2.2 collective-permute-start.8
  79.6 7.4 %collective-permute-done.24 = bf16[8,40,768]{2,1,0:T(8,128)(2,1)S(1)} collective-permute-done((bf16[8,40,768]{2,1,0:T(8,128)(2,1)}, bf16[8,40,768]{2,1,0:T(8,128)(2,1)S(1)}, u32[]{:S(2)}, u32[]{:S(2)}) %collective-permute-start.24) | collective-permute-done | bytes 491552 | tf_op jit(solution)/shard_map/ppermute | solution.py:17
  87.0 7.3 %collective-permute-start.9 = (bf16[4,40,768]{2,1,0:T(8,128)(2,1)S(1)}, bf16[4,40,768]{2,1,0:T(8,128)(2,1)S(1)}, u32[]{:S(2)}, u32[]{:S(2)}) collective-permute-start(bf16[4,40,768]{2,1,0:T(8,128)(2,1)S(1)} %collective-permute-done.7), channel_id=1, source_target_pairs={{0,224},{32,0},{64,32},{96,64},{128,96},{160,128},{192,160},{224,1... | collective-permute-start | bytes 737288 | tf_op jit(solution)/shard_map/ppermute | solution.py:17
  95.9 2.2 convolution_convert_fusion.1
  98.2 4.2 %collective-permute-start.10 = (bf16[4,40,384]{2,1,0:T(8,128)(2,1)S(1)}, bf16[4,40,384]{2,1,0:T(8,128)(2,1)S(1)}, u32[]{:S(2)}, u32[]{:S(2)}) collective-permute-start(bf16[4,40,384]{2,1,0:T(8,128)(2,1)S(1)} %slice.111), channel_id=1, source_target_pairs={{0,32},{32,64},{64,96},{96,128},{128,160},{160,192},{192,224},{224... | collective-permute-start | bytes 368648 | tf_op jit(solution)/shard_map/ppermute | solution.py:17
  102.4 13.9 %collective-permute-start.11 = (bf16[4,40,384]{2,1,0:T(8,128)(2,1)S(1)}, bf16[4,40,384]{2,1,0:T(8,128)(2,1)S(1)}, u32[]{:S(2)}, u32[]{:S(2)}) collective-permute-start(bf16[4,40,384]{2,1,0:T(8,128)(2,1)S(1)} %slice.112), channel_id=1, source_target_pairs={{0,224},{32,0},{64,32},{96,64},{128,96},{160,128},{192,160},{224,1... | collective-permute-start | bytes 368648 | tf_op jit(solution)/shard_map/ppermute | solution.py:17
  117.8 3.4 %collective-permute-done.11 = bf16[4,40,384]{2,1,0:T(8,128)(2,1)S(1)} collective-permute-done((bf16[4,40,384]{2,1,0:T(8,128)(2,1)S(1)}, bf16[4,40,384]{2,1,0:T(8,128)(2,1)S(1)}, u32[]{:S(2)}, u32[]{:S(2)}) %collective-permute-start.11) | collective-permute-done | bytes 122912 | tf_op jit(solution)/shard_map/ppermute | solution.py:17
  122.0 5.6 %convolution_convert_fusion.3 = bf16[640,512]{1,0:T(8,128)(2,1)} fusion(bf16[1280,768]{1,0:T(8,128)(2,1)} %bitcast.14, f32[640]{0:T(1024)S(1)} %copy-done.6, s32[1040]{0:T(1024)S(1)} %select_reduce_fusion.1, bf16[1024,1280]{1,0:T(8,128)(2,1)S(1)} %copy-done.2, bf16[16,1280]{1,0:T(8,128)(2,1)} %copy-done.8), kind=kOutput, calls=%fused_computation.32 | convolution fusion | flops 2550753280 | bytes 4635200 | tf_op jit(solution)/shard_map/dot_general | solution.py:104
  127.5 2.0 convolution_convert_fusion.2
  129.6 2.4 %convolution_multiply_fusion = f32[1040,512]{1,0:T(8,128)} fusion(bf16[640,512]{1,0:T(8,128)(2,1)S(1)} %copy-done.10, s32[1040]{0:T(1024)S(1)} %select_reduce_fusion.1, bf16[1040,256]{1,0:T(8,128)(2,1)S(1)} %slice-done, bf16[1040,256]{1,0:T(8,128)(2,1)S(1)} %convolution_convert_fusion.2), kind=kOutput, calls=%fused_computation.7 | convolution fusion | flops 684902400 | bytes 3854400 | tf_op jit(solution)/shard_map/dot_general | solution.py:112
  132.0 2.4 %reshape.100 = f32[1040,4,128]{2,1,0:T(4,128)S(1)} reshape(f32[1040,512]{1,0:T(8,128)} %convolution_multiply_fusion) | data formatting | bytes 4259840 | tf_op jit(solution)/shard_map/reshape | solution.py:116
  134.4 2.6 %reduce_sum.29 = f32[1040,4]{1,0:T(8,128)} reduce(f32[1040,4,128]{2,1,0:T(4,128)S(1)} %reshape.100, f32[]{:T(128)} %constant.113.clone.1), dimensions={2}, to_apply=%region_2.3 | reduce | flops 528320 | bytes 2146564 | tf_op jit(solution)/shard_map/reduce_sum | solution.py:116
  142.8 2.4 %mul.59 = f32[1040,4,128]{2,1,0:T(4,128)S(1)} broadcast(f32[1040,4]{1,0:T(8,128)S(1)} %copy.30), dimensions={0,1} | broadcast | bytes 2146560 | tf_op jit(solution)/shard_map/mul | solution.py:129
  145.2 3.6 %fusion.9 = f32[640,512]{1,0:T(8,128)} fusion(s32[1040]{0:T(1024)S(1)} %select_reduce_fusion.1, f32[130,8,4,128]{3,2,1,0:T(4,128)S(1)} %bitcast.95, bf16[1040,768]{1,0:T(8,128)(2,1)} %copy-done.4), kind=kOutput, calls=%fused_computation.20 | convolution fusion | flops 685434880 | bytes 4509760 | tf_op jit(solution)/shard_map/dot_general | solution.py:135
  149.7 5.0 %fusion.7 = bf16[1280,512]{1,0:T(8,128)(2,1)} fusion(s32[1280]{0:T(1024)S(1)} %iota_add_fusion, f32[80,8,4,128]{3,2,1,0:T(4,128)S(1)} %bitcast.98, f32[640,512]{1,0:T(8,128)} %fusion.9, f32[130,8,4,128]{3,2,1,0:T(4,128)S(1)} %bitcast.96, s32[1040]{0:T(1024)S(1)} %select_reduce_fusion.1, bf16[1040,768]{1,0:T(8,128)(2,1)} %copy-done.4), kind=kOutput, calls=%fused_computation.15 | convolution fusion | flops 1525155840 | bytes 7136320 | tf_op jit(solution)/shard_map/dot_general | solution.py:142
  155.9 1.9 collective-permute-start.27
  157.9 4.4 %collective-permute-start.28 = (bf16[256,512]{1,0:T(8,128)(2,1)S(1)}, bf16[256,512]{1,0:T(8,128)(2,1)S(1)}, u32[]{:S(2)}, u32[]{:S(2)}) collective-permute-start(bf16[256,512]{1,0:T(8,128)(2,1)S(1)} %get-tuple-element.13), channel_id=1, source_target_pairs={{8,0},{16,8},{24,16},{32,24},{40,32},{48,40},{56,48},{64,56},{72,6... | collective-permute-start | bytes 786440 | tf_op jit(solution)/shard_map/ppermute | solution.py:23
  162.2 3.6 %collective-permute-start.29 = (bf16[256,512]{1,0:T(8,128)(2,1)S(1)}, bf16[256,512]{1,0:T(8,128)(2,1)S(1)}, u32[]{:S(2)}, u32[]{:S(2)}) collective-permute-start(bf16[256,512]{1,0:T(8,128)(2,1)S(1)} %get-tuple-element.12), channel_id=1, source_target_pairs={{0,8},{8,16},{16,24},{24,32},{32,40},{40,48},{48,56},{56,64},{64,7... | collective-permute-start | bytes 786440 | tf_op jit(solution)/shard_map/ppermute | solution.py:23
  165.9 5.0 %collective-permute-start.30 = (bf16[256,512]{1,0:T(8,128)(2,1)S(1)}, bf16[256,512]{1,0:T(8,128)(2,1)S(1)}, u32[]{:S(2)}, u32[]{:S(2)}) collective-permute-start(bf16[256,512]{1,0:T(8,128)(2,1)S(1)} %get-tuple-element.11), channel_id=1, source_target_pairs={{0,16},{8,24},{16,32},{24,40},{32,48},{40,56},{48,64},{56,72},{64,... | collective-permute-start | bytes 786440 | tf_op jit(solution)/shard_map/ppermute | solution.py:23
  171.4 4.4 %collective-permute-done.30 = bf16[256,512]{1,0:T(8,128)(2,1)S(1)} collective-permute-done((bf16[256,512]{1,0:T(8,128)(2,1)S(1)}, bf16[256,512]{1,0:T(8,128)(2,1)S(1)}, u32[]{:S(2)}, u32[]{:S(2)}) %collective-permute-start.30) | collective-permute-done | bytes 262176 | tf_op jit(solution)/shard_map/ppermute | solution.py:23
  175.8 5.0 %convolution_convert_fusion = bf16[256,4096]{1,0:T(8,128)(2,1)} fusion(bf16[4096,512]{0,1:T(8,128)(2,1)} %all-gather.3.cloned.1.call-done, bf16[256,512]{1,0:T(8,128)(2,1)S(1)} %collective-permute-done.30, bf16[256,512]{1,0:T(8,128)(2,1)S(1)} %collective-permute-done.29, bf16[256,512]{1,0:T(8,128)(2,1)S(1)} %collective-permute-done.28, ...), kind=kOutput, calls=%fused_computation.6 | convolution fusion | flops 1076101120 | bytes 7602176 | tf_op jit(solution)/shard_map/dot_general | solution.py:151
  182.1 1.9 collective-permute-start.12
  184.0 2.2 collective-permute-start.13
  186.3 5.7 %collective-permute-start.14 = (bf16[256,512]{1,0:T(8,128)(2,1)S(1)}, bf16[256,512]{1,0:T(8,128)(2,1)S(1)}, u32[]{:S(2)}, u32[]{:S(2)}) collective-permute-start(bf16[256,512]{1,0:T(8,128)(2,1)S(1)} %get-tuple-element.8), channel_id=1, source_target_pairs={{0,8},{8,16},{16,24},{24,32},{32,40},{40,48},{48,56},{56,64},{64,7... | collective-permute-start | bytes 786440 | tf_op jit(solution)/shard_map/ppermute | solution.py:23
  192.0 4.2 %collective-permute-start.15 = (bf16[256,512]{1,0:T(8,128)(2,1)S(1)}, bf16[256,512]{1,0:T(8,128)(2,1)S(1)}, u32[]{:S(2)}, u32[]{:S(2)}) collective-permute-start(bf16[256,512]{1,0:T(8,128)(2,1)S(1)} %get-tuple-element.7), channel_id=1, source_target_pairs={{0,16},{8,24},{16,32},{24,40},{32,48},{40,56},{48,64},{56,72},{64,... | collective-permute-start | bytes 786440 | tf_op jit(solution)/shard_map/ppermute | solution.py:23
  196.2 4.9 %fusion.46 = f32[256,512]{1,0:T(8,128)} fusion(bf16[256,4096]{1,0:T(8,128)(2,1)} %all-gather.5.cloned.1.call-done, bf16[4096,512]{0,1:T(8,128)(2,1)} %all-gather.3.cloned.1.call-done), kind=kOutput, calls=%fused_computation.92 | convolution fusion | flops 1073741824 | bytes 6815744 | tf_op jit(solution)/shard_map/dot_general | solution.py:158
  202.4 19.0 %reduce-scatter.2.cloned.1.call-done = bf16[256,512]{1,0:T(8,128)(2,1)} async-done(((bf16[256,4096]{1,0:T(8,128)(2,1)}), bf16[256,512]{1,0:T(8,128)(2,1)}) %reduce-scatter.2.cloned.1.call-update) | async-done | bytes 262160 | tf_op jit(solution)/shard_map/reduce_scatter | solution.py:154
  221.4 1.9 add_convert_fusion
  (114 shorter events, 38.6 us)
Async XLA Ops:
  7.2 16.9 %copy-start.5 = (s32[1,1041]{1,0:T(1,128)S(1)}, s32[1,1041]{1,0:T(1,128)}, u32[]{:S(2)}) copy-start(s32[1,1041]{1,0:T(1,128)} %param.10) | copy-start | bytes 12496
  7.2 168.6 %all-gather.3.cloned.1.call-start = ((), (), s32[]{:S(2)}) async-start(), calls=%async_computation.1 | async-start | bytes 4325376 | tf_op jit(solution)/shard_map/all_gather | solution.py:69
  7.9 188.3 %all-gather.5.cloned.1.call-start = ((), (), s32[]{:S(2)}) async-start(), calls=%async_computation.3 | async-start | bytes 2359296 | tf_op jit(solution)/shard_map/all_gather | solution.py:159
  8.8 18.8 %copy-start = (bf16[1024,1280]{1,0:T(8,128)(2,1)S(1)}, bf16[1024,1280]{1,0:T(8,128)(2,1)}, u32[]{:S(2)}) copy-start(bf16[1024,1280]{1,0:T(8,128)(2,1)} %param.8) | copy-start | bytes 7864324
  10.5 32.6 %collective-permute-start.16 = (bf16[40,768]{1,0:T(8,128)(2,1)}, bf16[40,768]{1,0:T(8,128)(2,1)}, u32[]{:S(2)}, u32[]{:S(2)}) collective-permute-start(bf16[40,768]{1,0:T(8,128)(2,1)} %get-tuple-element.3), channel_id=1, source_target_pairs={{0,32},{32,64},{64,96},{96,128},{128,160},{160,192},{192,224},{224... | collective-permute-start | bytes 184328 | tf_op jit(solution)/shard_map/ppermute | solution.py:17
  12.4 32.3 %collective-permute-start.17 = (bf16[40,768]{1,0:T(8,128)(2,1)}, bf16[40,768]{1,0:T(8,128)(2,1)}, u32[]{:S(2)}, u32[]{:S(2)}) collective-permute-start(bf16[40,768]{1,0:T(8,128)(2,1)} %get-tuple-element.3), channel_id=1, source_target_pairs={{0,224},{32,0},{64,32},{96,64},{128,96},{160,128},{192,160},{224,1... | collective-permute-start | bytes 184328 | tf_op jit(solution)/shard_map/ppermute | solution.py:17
  16.3 16.0 %collective-permute-start.1 = (bf16[40,768]{1,0:T(8,128)(2,1)}, bf16[40,768]{1,0:T(8,128)(2,1)}, u32[]{:S(2)}, u32[]{:S(2)}) collective-permute-start(bf16[40,768]{1,0:T(8,128)(2,1)} %get-tuple-element.15), channel_id=1, source_target_pairs={{0,8},{8,16},{16,24},{24,0},{1,9},{9,17},{17,25},{25,1},{2,10},{10... | collective-permute-start | bytes 184328 | tf_op jit(solution)/shard_map/ppermute | solution.py:17
  16.8 19.1 %collective-permute-start.2 = (bf16[40,768]{1,0:T(8,128)(2,1)}, bf16[40,768]{1,0:T(8,128)(2,1)}, u32[]{:S(2)}, u32[]{:S(2)}) collective-permute-start(bf16[40,768]{1,0:T(8,128)(2,1)} %get-tuple-element.15), channel_id=1, source_target_pairs={{0,16},{8,24},{16,0},{24,8},{1,17},{9,25},{17,1},{25,9},{2,18},{10... | collective-permute-start | bytes 184328 | tf_op jit(solution)/shard_map/ppermute | solution.py:17
  19.2 17.5 %collective-permute-start.3 = (bf16[40,768]{1,0:T(8,128)(2,1)}, bf16[40,768]{1,0:T(8,128)(2,1)}, u32[]{:S(2)}, u32[]{:S(2)}) collective-permute-start(bf16[40,768]{1,0:T(8,128)(2,1)} %get-tuple-element.15), channel_id=1, source_target_pairs={{0,24},{8,0},{16,8},{24,16},{1,25},{9,1},{17,9},{25,17},{2,26},{10... | collective-permute-start | bytes 184328 | tf_op jit(solution)/shard_map/ppermute | solution.py:17
  19.3 202.2 %reduce-scatter.2.cloned.1.call-start = ((), (), s32[]{:S(2)}) async-start(), calls=%async_computation.2 | async-start | bytes 2359296 | tf_op jit(solution)/shard_map/reduce_scatter | solution.py:154
  29.0 1.6 copy-start.1
  32.4 63.5 %collective-permute-start = (bf16[16,1280]{1,0:T(8,128)(2,1)}, bf16[16,1280]{1,0:T(8,128)(2,1)S(1)}, u32[]{:S(2)}, u32[]{:S(2)}) collective-permute-start(bf16[16,1280]{1,0:T(8,128)(2,1)} %slice.110), channel_id=1, source_target_pairs={{0,8},{8,16},{16,24},{24,32},{32,40},{40,48},{48,56},{56,64},{64,7... | collective-permute-start | bytes 122888 | tf_op jit(solution)/shard_map/ppermute | solution.py:23
  37.6 27.4 %collective-permute-start.4 = (bf16[4,40,768]{2,1,0:T(8,128)(2,1)S(1)}, bf16[4,40,768]{2,1,0:T(8,128)(2,1)S(1)}, u32[]{:S(2)}, u32[]{:S(2)}) collective-permute-start(bf16[4,40,768]{2,1,0:T(8,128)(2,1)S(1)} %bitcast_dynamic-update-slice_fusion.18), channel_id=1, source_target_pairs={{0,32},{32,64},{64,96},{96,128},{128,160},{160,192},{192,224},{224... | collective-permute-start | bytes 737288 | tf_op jit(solution)/shard_map/ppermute | solution.py:17
  39.5 26.3 %collective-permute-start.5 = (bf16[4,40,768]{2,1,0:T(8,128)(2,1)S(1)}, bf16[4,40,768]{2,1,0:T(8,128)(2,1)S(1)}, u32[]{:S(2)}, u32[]{:S(2)}) collective-permute-start(bf16[4,40,768]{2,1,0:T(8,128)(2,1)S(1)} %bitcast_dynamic-update-slice_fusion.18), channel_id=1, source_target_pairs={{0,224},{32,0},{64,32},{96,64},{128,96},{160,128},{192,160},{224,1... | collective-permute-start | bytes 737288 | tf_op jit(solution)/shard_map/ppermute | solution.py:17
  43.0 6.2 %collective-permute-start.18 = (bf16[40,768]{1,0:T(8,128)(2,1)}, bf16[40,768]{1,0:T(8,128)(2,1)S(1)}, u32[]{:S(2)}, u32[]{:S(2)}) collective-permute-start(bf16[40,768]{1,0:T(8,128)(2,1)} %collective-permute-done.16), channel_id=1, source_target_pairs={{0,32},{32,64},{64,96},{96,128},{128,160},{160,192},{192,224},{224... | collective-permute-start | bytes 184328 | tf_op jit(solution)/shard_map/ppermute | solution.py:17
  44.7 6.2 %collective-permute-start.19 = (bf16[40,768]{1,0:T(8,128)(2,1)}, bf16[40,768]{1,0:T(8,128)(2,1)S(1)}, u32[]{:S(2)}, u32[]{:S(2)}) collective-permute-start(bf16[40,768]{1,0:T(8,128)(2,1)} %collective-permute-done.17), channel_id=1, source_target_pairs={{0,224},{32,0},{64,32},{96,64},{128,96},{160,128},{192,160},{224,1... | collective-permute-start | bytes 184328 | tf_op jit(solution)/shard_map/ppermute | solution.py:17
  49.2 5.4 %collective-permute-start.20 = (bf16[40,768]{1,0:T(8,128)(2,1)S(1)}, bf16[40,768]{1,0:T(8,128)(2,1)S(1)}, u32[]{:S(2)}, u32[]{:S(2)}) collective-permute-start(bf16[40,768]{1,0:T(8,128)(2,1)S(1)} %collective-permute-done.18), channel_id=1, source_target_pairs={{0,32},{32,64},{64,96},{96,128},{128,160},{160,192},{192,224},{224... | collective-permute-start | bytes 184328 | tf_op jit(solution)/shard_map/ppermute | solution.py:17
  50.9 4.6 %collective-permute-start.21 = (bf16[40,768]{1,0:T(8,128)(2,1)S(1)}, bf16[40,768]{1,0:T(8,128)(2,1)S(1)}, u32[]{:S(2)}, u32[]{:S(2)}) collective-permute-start(bf16[40,768]{1,0:T(8,128)(2,1)S(1)} %collective-permute-done.19), channel_id=1, source_target_pairs={{0,224},{32,0},{64,32},{96,64},{128,96},{160,128},{192,160},{224,1... | collective-permute-start | bytes 184328 | tf_op jit(solution)/shard_map/ppermute | solution.py:17
  54.6 5.1 %collective-permute-start.22 = (bf16[40,384]{1,0:T(8,128)(2,1)S(1)}, bf16[40,384]{1,0:T(8,128)(2,1)S(1)}, u32[]{:S(2)}, u32[]{:S(2)}) collective-permute-start(bf16[40,384]{1,0:T(8,128)(2,1)S(1)} %slice.120), channel_id=1, source_target_pairs={{0,32},{32,64},{64,96},{96,128},{128,160},{160,192},{192,224},{224... | collective-permute-start | bytes 92168 | tf_op jit(solution)/shard_map/ppermute | solution.py:17
  55.4 4.3 %collective-permute-start.23 = (bf16[40,384]{1,0:T(8,128)(2,1)S(1)}, bf16[40,384]{1,0:T(8,128)(2,1)S(1)}, u32[]{:S(2)}, u32[]{:S(2)}) collective-permute-start(bf16[40,384]{1,0:T(8,128)(2,1)S(1)} %slice.121), channel_id=1, source_target_pairs={{0,224},{32,0},{64,32},{96,64},{128,96},{160,128},{192,160},{224,1... | collective-permute-start | bytes 92168 | tf_op jit(solution)/shard_map/ppermute | solution.py:17
  60.4 26.6 %collective-permute-start.24 = (bf16[8,40,768]{2,1,0:T(8,128)(2,1)}, bf16[8,40,768]{2,1,0:T(8,128)(2,1)S(1)}, u32[]{:S(2)}, u32[]{:S(2)}) collective-permute-start(bf16[8,40,768]{2,1,0:T(8,128)(2,1)} %fusion.37), channel_id=1, source_target_pairs={{0,8},{8,16},{16,24},{24,0},{1,9},{9,17},{17,25},{25,1},{2,10},{10... | collective-permute-start | bytes 1474568 | tf_op jit(solution)/shard_map/ppermute | solution.py:17
  63.4 31.0 %collective-permute-start.25 = (bf16[8,40,768]{2,1,0:T(8,128)(2,1)}, bf16[8,40,768]{2,1,0:T(8,128)(2,1)S(1)}, u32[]{:S(2)}, u32[]{:S(2)}) collective-permute-start(bf16[8,40,768]{2,1,0:T(8,128)(2,1)} %fusion.37), channel_id=1, source_target_pairs={{0,16},{8,24},{16,0},{24,8},{1,17},{9,25},{17,1},{25,9},{2,18},{10... | collective-permute-start | bytes 1474568 | tf_op jit(solution)/shard_map/ppermute | solution.py:17
  65.0 7.9 %collective-permute-start.6 = (bf16[4,40,768]{2,1,0:T(8,128)(2,1)S(1)}, bf16[4,40,768]{2,1,0:T(8,128)(2,1)S(1)}, u32[]{:S(2)}, u32[]{:S(2)}) collective-permute-start(bf16[4,40,768]{2,1,0:T(8,128)(2,1)S(1)} %collective-permute-done.4), channel_id=1, source_target_pairs={{0,32},{32,64},{64,96},{96,128},{128,160},{160,192},{192,224},{224... | collective-permute-start | bytes 737288 | tf_op jit(solution)/shard_map/ppermute | solution.py:17
  65.8 30.1 %copy-start.2 = (bf16[1024,1280]{1,0:T(8,128)(2,1)S(1)}, bf16[1024,1280]{1,0:T(8,128)(2,1)}, u32[]{:S(2)}) copy-start(bf16[1024,1280]{1,0:T(8,128)(2,1)} %copy-done.1) | copy-start | bytes 7864324
  65.8 10.9 %collective-permute-start.7 = (bf16[4,40,768]{2,1,0:T(8,128)(2,1)S(1)}, bf16[4,40,768]{2,1,0:T(8,128)(2,1)S(1)}, u32[]{:S(2)}, u32[]{:S(2)}) collective-permute-start(bf16[4,40,768]{2,1,0:T(8,128)(2,1)S(1)} %collective-permute-done.5), channel_id=1, source_target_pairs={{0,224},{32,0},{64,32},{96,64},{128,96},{160,128},{192,160},{224,1... | collective-permute-start | bytes 737288 | tf_op jit(solution)/shard_map/ppermute | solution.py:17
  72.9 22.9 %collective-permute-start.26 = (bf16[8,40,768]{2,1,0:T(8,128)(2,1)}, bf16[8,40,768]{2,1,0:T(8,128)(2,1)S(1)}, u32[]{:S(2)}, u32[]{:S(2)}) collective-permute-start(bf16[8,40,768]{2,1,0:T(8,128)(2,1)} %fusion.37), channel_id=1, source_target_pairs={{0,24},{8,0},{16,8},{24,16},{1,25},{9,1},{17,9},{25,17},{2,26},{10... | collective-permute-start | bytes 1474568 | tf_op jit(solution)/shard_map/ppermute | solution.py:17
  76.7 21.5 %collective-permute-start.8 = (bf16[4,40,768]{2,1,0:T(8,128)(2,1)S(1)}, bf16[4,40,768]{2,1,0:T(8,128)(2,1)S(1)}, u32[]{:S(2)}, u32[]{:S(2)}) collective-permute-start(bf16[4,40,768]{2,1,0:T(8,128)(2,1)S(1)} %collective-permute-done.6), channel_id=1, source_target_pairs={{0,32},{32,64},{64,96},{96,128},{128,160},{160,192},{192,224},{224... | collective-permute-start | bytes 737288 | tf_op jit(solution)/shard_map/ppermute | solution.py:17
  87.0 15.4 %collective-permute-start.9 = (bf16[4,40,768]{2,1,0:T(8,128)(2,1)S(1)}, bf16[4,40,768]{2,1,0:T(8,128)(2,1)S(1)}, u32[]{:S(2)}, u32[]{:S(2)}) collective-permute-start(bf16[4,40,768]{2,1,0:T(8,128)(2,1)S(1)} %collective-permute-done.7), channel_id=1, source_target_pairs={{0,224},{32,0},{64,32},{96,64},{128,96},{160,128},{192,160},{224,1... | collective-permute-start | bytes 737288 | tf_op jit(solution)/shard_map/ppermute | solution.py:17
  95.9 2.3 copy-start.8
  98.1 19.6 %copy-start.4 = (bf16[1040,768]{1,0:T(8,128)(2,1)}, bf16[1040,768]{1,0:T(8,128)(2,1)S(1)}, u32[]{:S(2)}) copy-start(bf16[1040,768]{1,0:T(8,128)(2,1)S(1)} %convolution_convert_fusion.1) | copy-start | bytes 4792324
  98.2 23.8 %copy-start.6 = (f32[640]{0:T(1024)S(1)}, f32[640]{0:T(1024)}, u32[]{:S(2)}) copy-start(f32[640]{0:T(1024)} %compare_select_fusion.1) | copy-start | bytes 7684
  98.2 19.6 %collective-permute-start.10 = (bf16[4,40,384]{2,1,0:T(8,128)(2,1)S(1)}, bf16[4,40,384]{2,1,0:T(8,128)(2,1)S(1)}, u32[]{:S(2)}, u32[]{:S(2)}) collective-permute-start(bf16[4,40,384]{2,1,0:T(8,128)(2,1)S(1)} %slice.111), channel_id=1, source_target_pairs={{0,32},{32,64},{64,96},{96,128},{128,160},{160,192},{192,224},{224... | collective-permute-start | bytes 368648 | tf_op jit(solution)/shard_map/ppermute | solution.py:17
  102.4 18.8 %collective-permute-start.11 = (bf16[4,40,384]{2,1,0:T(8,128)(2,1)S(1)}, bf16[4,40,384]{2,1,0:T(8,128)(2,1)S(1)}, u32[]{:S(2)}, u32[]{:S(2)}) collective-permute-start(bf16[4,40,384]{2,1,0:T(8,128)(2,1)S(1)} %slice.112), channel_id=1, source_target_pairs={{0,224},{32,0},{64,32},{96,64},{128,96},{160,128},{192,160},{224,1... | collective-permute-start | bytes 368648 | tf_op jit(solution)/shard_map/ppermute | solution.py:17
  122.0 5.6 %copy-start.9 = (bf16[16,1280]{1,0:T(8,128)(2,1)S(1)}, bf16[16,1280]{1,0:T(8,128)(2,1)}, u32[]{:S(2)}) copy-start(bf16[16,1280]{1,0:T(8,128)(2,1)} %copy-done.8) | copy-start | bytes 122884
  127.5 2.1 slice-start
  127.5 2.1 copy-start.10
  134.4 4.9 %copy-start.7 = (pred[1040]{0:T(1024)(128)(4,1)S(1)}, pred[1040]{0:T(1024)(128)(4,1)}, u32[]{:S(2)}) copy-start(pred[1040]{0:T(1024)(128)(4,1)} %fusion.38) | copy-start | bytes 3124
  145.2 3.7 %copy-start.3 = (f32[640,4]{1,0:T(8,128)S(1)}, f32[640,4]{1,0:T(8,128)}, u32[]{:S(2)}) copy-start(f32[640,4]{1,0:T(8,128)} %copy.31) | copy-start | bytes 30724
  155.9 14.9 %collective-permute-start.27 = (bf16[256,512]{1,0:T(8,128)(2,1)S(1)}, bf16[256,512]{1,0:T(8,128)(2,1)S(1)}, u32[]{:S(2)}, u32[]{:S(2)}) collective-permute-start(bf16[256,512]{1,0:T(8,128)(2,1)S(1)} %get-tuple-element.10), channel_id=1, source_target_pairs={{16,0},{24,8},{32,16},{40,24},{48,32},{56,40},{64,48},{72,56},{80,... | collective-permute-start | bytes 786440 | tf_op jit(solution)/shard_map/ppermute | solution.py:23
  157.9 13.5 %collective-permute-start.28 = (bf16[256,512]{1,0:T(8,128)(2,1)S(1)}, bf16[256,512]{1,0:T(8,128)(2,1)S(1)}, u32[]{:S(2)}, u32[]{:S(2)}) collective-permute-start(bf16[256,512]{1,0:T(8,128)(2,1)S(1)} %get-tuple-element.13), channel_id=1, source_target_pairs={{8,0},{16,8},{24,16},{32,24},{40,32},{48,40},{56,48},{64,56},{72,6... | collective-permute-start | bytes 786440 | tf_op jit(solution)/shard_map/ppermute | solution.py:23
  162.2 9.2 %collective-permute-start.29 = (bf16[256,512]{1,0:T(8,128)(2,1)S(1)}, bf16[256,512]{1,0:T(8,128)(2,1)S(1)}, u32[]{:S(2)}, u32[]{:S(2)}) collective-permute-start(bf16[256,512]{1,0:T(8,128)(2,1)S(1)} %get-tuple-element.12), channel_id=1, source_target_pairs={{0,8},{8,16},{16,24},{24,32},{32,40},{40,48},{48,56},{56,64},{64,7... | collective-permute-start | bytes 786440 | tf_op jit(solution)/shard_map/ppermute | solution.py:23
  165.9 14.9 %copy-start.11 = (bf16[640,512]{1,0:T(8,128)(2,1)S(1)}, bf16[640,512]{1,0:T(8,128)(2,1)}, u32[]{:S(2)}) copy-start(bf16[640,512]{1,0:T(8,128)(2,1)} %convolution_convert_fusion.3) | copy-start | bytes 1966084
  165.9 9.9 %collective-permute-start.30 = (bf16[256,512]{1,0:T(8,128)(2,1)S(1)}, bf16[256,512]{1,0:T(8,128)(2,1)S(1)}, u32[]{:S(2)}, u32[]{:S(2)}) collective-permute-start(bf16[256,512]{1,0:T(8,128)(2,1)S(1)} %get-tuple-element.11), channel_id=1, source_target_pairs={{0,16},{8,24},{16,32},{24,40},{32,48},{40,56},{48,64},{56,72},{64,... | collective-permute-start | bytes 786440 | tf_op jit(solution)/shard_map/ppermute | solution.py:23
  182.1 19.1 %collective-permute-start.12 = (bf16[256,512]{1,0:T(8,128)(2,1)S(1)}, bf16[256,512]{1,0:T(8,128)(2,1)S(1)}, u32[]{:S(2)}, u32[]{:S(2)}) collective-permute-start(bf16[256,512]{1,0:T(8,128)(2,1)S(1)} %get-tuple-element.6), channel_id=1, source_target_pairs={{16,0},{24,8},{32,16},{40,24},{48,32},{56,40},{64,48},{72,56},{80,... | collective-permute-start | bytes 786440 | tf_op jit(solution)/shard_map/ppermute | solution.py:23
  184.0 17.2 %collective-permute-start.13 = (bf16[256,512]{1,0:T(8,128)(2,1)S(1)}, bf16[256,512]{1,0:T(8,128)(2,1)S(1)}, u32[]{:S(2)}, u32[]{:S(2)}) collective-permute-start(bf16[256,512]{1,0:T(8,128)(2,1)S(1)} %get-tuple-element.9), channel_id=1, source_target_pairs={{8,0},{16,8},{24,16},{32,24},{40,32},{48,40},{56,48},{64,56},{72,6... | collective-permute-start | bytes 786440 | tf_op jit(solution)/shard_map/ppermute | solution.py:23
  186.3 14.9 %collective-permute-start.14 = (bf16[256,512]{1,0:T(8,128)(2,1)S(1)}, bf16[256,512]{1,0:T(8,128)(2,1)S(1)}, u32[]{:S(2)}, u32[]{:S(2)}) collective-permute-start(bf16[256,512]{1,0:T(8,128)(2,1)S(1)} %get-tuple-element.8), channel_id=1, source_target_pairs={{0,8},{8,16},{16,24},{24,32},{32,40},{40,48},{48,56},{56,64},{64,7... | collective-permute-start | bytes 786440 | tf_op jit(solution)/shard_map/ppermute | solution.py:23
  192.0 10.5 %collective-permute-start.15 = (bf16[256,512]{1,0:T(8,128)(2,1)S(1)}, bf16[256,512]{1,0:T(8,128)(2,1)S(1)}, u32[]{:S(2)}, u32[]{:S(2)}) collective-permute-start(bf16[256,512]{1,0:T(8,128)(2,1)S(1)} %get-tuple-element.7), channel_id=1, source_target_pairs={{0,16},{8,24},{16,32},{24,40},{32,48},{40,56},{48,64},{56,72},{64,... | collective-permute-start | bytes 786440 | tf_op jit(solution)/shard_map/ppermute | solution.py:23
Sparse Core Ops, SparseCore 0:
  10.5 101.0 all-gather.2
  113.4 26.5 all-gather.4
  180.9 40.4 reduce-scatter.1
